TPU v7x, 512 devices: a whole 4x8x8 slice. The times are simulated.
512 devices in a mesh: expert: 8 (over x, core), hidden: 64 (over y, z).
Axes of the slice: x: 4, y: 8, z: 8, core: 2. Of those that a mesh axis runs over, the one named last changes fastest.
Arguments:
- tokens: bfloat16 [1024, 3072], P('expert', 'hidden'), may hold values from -6 to 6
- grad_out: bfloat16 [1024, 3072], P('expert', 'hidden'), may hold values from -6 to 6
- lang_ids: int32 [1024, 1], P('expert'), may hold values from 0 to 7; in each aligned block of 128 rows (0 to 127, 128 to 255, ...) at most 40 rows name the same one
- gate_weight: bfloat16 [8, 3072, 8192], P('expert', None, 'hidden'), may hold values from -0.3125 to 0.3125
- up_weight: bfloat16 [8, 3072, 8192], P('expert', None, 'hidden'), may hold values from -0.109375 to 0.109375
- down_weight: bfloat16 [8, 8192, 3072], P('expert', 'hidden'), may hold values from -0.0625 to 0.0625
Outputs:
- grad_tokens: bfloat16 [1024, 3072], P('expert', 'hidden')
- grad_gate: bfloat16 [8, 3072, 8192], P('expert', None, 'hidden')
- grad_up: bfloat16 [8, 3072, 8192], P('expert', None, 'hidden')
- grad_down: bfloat16 [8, 8192, 3072], P('expert', 'hidden')
Inputs may be any that keep to these rules, and one draw needn't show every extreme that they name: `lang_ids`: in each aligned block of 128 tokens at most 40 tokens name one expert; some block reaches 40. Every expert is named by some token.
All inputs are finite; a program needn't handle non-finite values.
Results may differ from a plain program's by a relative error of at most 0.005.
Values may be sent and summed in bfloat16 or wider, within the bound.
A program may use at most 64 MiB of HBM per device.

v0:
```python
import jax
import jax.numpy as jnp
from jax import lax
from jax.sharding import PartitionSpec as P


def contract_rows(left, right):
    return lax.dot_general(
        left, right, (((0,), (0,)), ((), ())), preferred_element_type=jnp.float32
    )


def contract_cols(left, right):
    return lax.dot_general(
        left, right, (((1,), (1,)), ((), ())), preferred_element_type=jnp.float32
    )


def slot_index(expert_ids, count):
    onehot = (expert_ids[:, None] == jnp.arange(count, dtype=jnp.int32)[None, :]).astype(jnp.int32)
    before = jnp.cumsum(onehot, axis=0) - onehot
    return jnp.sum(before * onehot, axis=1)


def expert_backward(x_rows, dy_rows, w_gate, w_up, w_down):
    gate_pre = jnp.dot(x_rows, w_gate, preferred_element_type=jnp.float32)
    up_pre = jnp.dot(x_rows, w_up, preferred_element_type=jnp.float32)
    sigma_gate = jax.nn.sigmoid(gate_pre)
    activated = gate_pre * sigma_gate
    hidden = (activated * up_pre).astype(jnp.bfloat16)
    d_hidden = contract_cols(dy_rows, w_down)
    d_up = (d_hidden * activated).astype(jnp.bfloat16)
    d_gate = (d_hidden * up_pre * sigma_gate * (1.0 + gate_pre * (1.0 - sigma_gate))).astype(
        jnp.bfloat16
    )
    grad_gate = contract_rows(x_rows, d_gate).astype(jnp.bfloat16)
    grad_up = contract_rows(x_rows, d_up).astype(jnp.bfloat16)
    grad_down = contract_rows(hidden, dy_rows).astype(jnp.bfloat16)
    partial_sum = contract_cols(d_gate, w_gate) + contract_cols(d_up, w_up)
    return (grad_gate, grad_up, grad_down, partial_sum)


def local(tokens, grad_out, lang_ids, gate_weight, up_weight, down_weight):
    groups = lax.axis_size("expert")
    tok_rows = tokens.shape[0]
    capacity = min(tok_rows, 5 * tok_rows // (2 * groups))
    expert_ids = lang_ids[:, 0]
    slots = slot_index(expert_ids, groups)

    def place(values):
        empty = jnp.zeros((groups, capacity, values.shape[1]), values.dtype)
        return empty.at[expert_ids, slots].set(values)

    x_blocks, dy_blocks = (
        lax.all_to_all(place(tokens), "expert", split_axis=0, concat_axis=0, tiled=True),
        lax.all_to_all(place(grad_out), "expert", split_axis=0, concat_axis=0, tiled=True),
    )
    x_blocks, dy_blocks = (
        lax.all_gather(x_blocks, "hidden", axis=2, tiled=True),
        lax.all_gather(dy_blocks, "hidden", axis=2, tiled=True),
    )
    row_count = groups * capacity
    width = x_blocks.shape[2]
    x_rows = x_blocks.reshape(row_count, width)
    dy_rows = dy_blocks.reshape(row_count, width)
    grad_gate, grad_up, grad_down, partial_sum = expert_backward(
        x_rows, dy_rows, gate_weight[0], up_weight[0], down_weight[0]
    )
    partial_blocks = partial_sum.reshape(groups, capacity, width)
    summed = lax.psum_scatter(partial_blocks, "hidden", scatter_dimension=2, tiled=True)
    back_rows = lax.all_to_all(
        summed.astype(jnp.bfloat16), "expert", split_axis=0, concat_axis=0, tiled=True
    )
    grad_tokens = back_rows[expert_ids, slots]
    return (grad_tokens, grad_gate[None], grad_up[None], grad_down[None])


def solution(mesh):
    in_specs = (
        P("expert", "hidden"),
        P("expert", "hidden"),
        P("expert", None),
        P("expert", None, "hidden"),
        P("expert", None, "hidden"),
        P("expert", "hidden", None),
    )
    out_specs = (
        P("expert", "hidden"),
        P("expert", None, "hidden"),
        P("expert", None, "hidden"),
        P("expert", "hidden", None),
    )
    return jax.shard_map(local, mesh=mesh, in_specs=in_specs, out_specs=out_specs, check_vma=False)
```

profile of v0, /device:TPU:1, one launch (start us, length us, event | category | flops | bytes accessed | tf_op | source)
XLA Modules:
  0.0 574.6 jit_solution(13738326081188786696)
XLA Ops:
  7.2 0.9 copy.22
  9.0 0.8 select_reduce_fusion
  10.6 7.1 %scatter_fusion.1 = bf16[8,40,48]{2,1,0:T(8,128)(2,1)S(1)} fusion(bf16[8,40,48]{2,1,0:T(8,128)(2,1)S(1)} %broadcast.34.clone, s32[128]{0:T(128)S(1)} %get-tuple-element.20, bf16[128,48]{1,0:T(8,128)(2,1)S(1)} %copy.22), kind=kCustom, calls=%fused_computation.2 | custom fusion | bytes 37888 | tf_op jit(solution)/shard_map/scatter | solution.py:52
  17.8 14.0 %all_to_all.15 = bf16[8,2,960]{2,1,0:T(2,128)(2,1)S(1)} all-to-all(bf16[8,2,960]{2,1,0:T(2,128)(2,1)S(1)} %reshape.54), channel_id=1, replica_groups=mesh['expert'=8,'hidden'=64] {'expert'}, dimensions={0} | all-to-all | bytes 61440 | tf_op jit(solution)/shard_map/all_to_all | solution.py:55
  31.9 0.8 copy.23
  32.7 0.8 copy.19
  33.6 7.1 %scatter_fusion = bf16[8,40,48]{2,1,0:T(8,128)(2,1)S(1)} fusion(bf16[8,40,48]{2,1,0:T(8,128)(2,1)S(1)} %broadcast.34.clone.1, s32[128]{0:T(128)S(1)} %get-tuple-element.20, bf16[128,48]{1,0:T(8,128)(2,1)S(1)} %copy.19), kind=kCustom, calls=%fused_computation.1 | custom fusion | bytes 37888 | tf_op jit(solution)/shard_map/scatter | solution.py:52
  40.8 7.8 %all_to_all.16 = bf16[8,2,960]{2,1,0:T(2,128)(2,1)S(1)} all-to-all(bf16[8,2,960]{2,1,0:T(2,128)(2,1)S(1)} %reshape.56), channel_id=1, replica_groups=mesh['expert'=8,'hidden'=64] {'expert'}, dimensions={0} | all-to-all | bytes 61440 | tf_op jit(solution)/shard_map/all_to_all | solution.py:56
  49.6 1.3 dynamic-slice
  51.5 70.7 %all-gather.5.cloned.1.call-done = bf16[8,40,3072]{1,0,2:T(8,128)(2,1)} async-done(((bf16[8,40,48]{1,0,2:T(8,128)(2,1)}), bf16[8,40,3072]{1,0,2:T(8,128)(2,1)}) %all-gather.5.cloned.1.call-update) | async-done | bytes 1966096 | tf_op jit(solution)/shard_map/all_gather | solution.py:59
  122.2 6.4 %copy.24 = bf16[8,40,3072]{2,1,0:T(8,128)(2,1)S(1)} copy(bf16[8,40,3072]{1,0,2:T(8,128)(2,1)} %all-gather.5.cloned.1.call-done) | data formatting | bytes 3932160 | tf_op jit(solution)/shard_map/all_gather | solution.py:59
  128.6 1.4 fusion.5
  129.9 1.3 fusion.8
  131.3 81.4 %all-gather.3.cloned.1.call-done = bf16[8,40,3072]{1,0,2:T(8,128)(2,1)} async-done(((bf16[8,40,48]{1,0,2:T(8,128)(2,1)}), bf16[8,40,3072]{1,0,2:T(8,128)(2,1)}) %all-gather.3.cloned.1.call-update) | async-done | bytes 1966096 | tf_op jit(solution)/shard_map/all_gather | solution.py:60
  212.7 7.4 %copy.21 = bf16[8,40,3072]{2,1,0:T(8,128)(2,1)} copy(bf16[8,40,3072]{1,0,2:T(8,128)(2,1)} %all-gather.3.cloned.1.call-done) | data formatting | bytes 3932160 | tf_op jit(solution)/shard_map/all_gather | solution.py:60
  220.1 3.4 fusion.2
  224.2 1.7 fusion.1
  226.6 2.5 convolution_add_fusion
  229.2 270.8 %all-reduce.2 = bf16[8,40,3072]{2,1,0:T(8,128)(2,1)} all-reduce(f32[8,40,3072]{2,1,0:T(8,128)} %bitcast.54), channel_id=2, replica_groups=mesh['expert'=8,'hidden'=64] {'hidden'}, use_global_device_ids=true, to_apply=%region_4.5.clone | all-reduce | flops 983040 | bytes 5898240
  500.0 1.0 dynamic-slice_convert_fusion
  501.8 59.3 %all-to-all-start.2 = ((bf16[8,2,960]{2,1,0:T(2,128)(2,1)}), bf16[8,2,960]{2,1,0:T(2,128)(2,1)S(1)}, u32[]{:S(2)}, u32[]{:S(2)}) async-start(bf16[8,2,960]{2,1,0:T(2,128)(2,1)} %reshape.58), calls=%async_computation.2 | async-start | bytes 65536 | tf_op jit(solution)/shard_map/all_to_all | solution.py:71
  561.1 1.7 fusion
  562.9 3.0 all-to-all-done.2
  566.0 1.1 gather_fusion
  (35 shorter events, 6.0 us)
Async XLA Ops:
  7.2 121.4 %copy-start = (bf16[1,3072,128]{2,1,0:T(8,128)(2,1)S(1)}, bf16[1,3072,128]{2,1,0:T(8,128)(2,1)}, u32[]{:S(2)}) copy-start(bf16[1,3072,128]{2,1,0:T(8,128)(2,1)} %param.9) | copy-start | bytes 2359300
  7.2 115.0 %all-gather.5.cloned.1.call-start = ((), (), s32[]{:S(2)}) async-start(), calls=%async_computation.4 | async-start | bytes 6389760 | tf_op jit(solution)/shard_map/all_gather | solution.py:59
  32.7 180.0 %all-gather.3.cloned.1.call-start = ((), (), s32[]{:S(2)}) async-start(), calls=%async_computation.3 | async-start | bytes 6389760 | tf_op jit(solution)/shard_map/all_gather | solution.py:60
  128.6 1.4 copy-start.2
  220.1 3.4 copy-start.1
  220.1 3.4 copy-start.3
  220.1 3.4 copy-start.4
  220.1 3.4 copy-start.7
  224.2 1.7 copy-start.5
  229.2 331.9 %copy-start.6 = (bf16[320,128]{1,0:T(8,128)(2,1)S(1)}, bf16[320,128]{1,0:T(8,128)(2,1)}, u32[]{:S(2)}) copy-start(bf16[320,128]{1,0:T(8,128)(2,1)} %copy-done.5) | copy-start | bytes 245764
  501.8 64.1 %all-to-all-start.2 = ((bf16[8,2,960]{2,1,0:T(2,128)(2,1)}), bf16[8,2,960]{2,1,0:T(2,128)(2,1)S(1)}, u32[]{:S(2)}, u32[]{:S(2)}) async-start(bf16[8,2,960]{2,1,0:T(2,128)(2,1)} %reshape.58), calls=%async_computation.2 | async-start | bytes 65536 | tf_op jit(solution)/shard_map/all_to_all | solution.py:71
Sparse Core Ops, SparseCore 0:
  32.8 89.3 all-gather.4
  125.2 87.4 all-gather.2
where the time goes:
time: 575 us
  blocking collectives  293 us (51%)
  waiting for transfers between devices  155 us (27%)
  starting transfers between devices  59.4 us (10%)
  local copies, waits for them, and re-layouts  36.8 us (6%)
  between operations  14.8 us (3%)
  matrix products  13.4 us (2%)
    unnamed x1, blocking collectives  271 us
    all_gather x1, waiting for transfers between devices, local(): lax.all_gather(dy_blocks, 'hidden', axis=2, tiled=True)  81.4 us
    all_gather x1, waiting for transfers between devices, local(): lax.all_gather(x_blocks, 'hidden', axis=2, tiled=True)  70.7 us
    all_to_all x1, starting transfers between devices, local(): lax.all_to_all(summed.astype(jnp.bfloat16), 'expert', split_axis=0, conca...  59.3 us
    scatter x2, local copies, waits for them, and re-layouts, place(): return empty.at[expert_ids, slots].set(values)  14.2 us
    all_to_all x1, blocking collectives, local(): lax.all_to_all(place(tokens), 'expert', split_axis=0, concat_axis=0, tile...  14 us
  transfers between devices with their start and end apart: 3, of which 3 were waited for; matrix products, arithmetic and copies ran while one was open for 4% of the time, Pallas kernels for 0%

commit v1 on v0

v1 whole, which is shorter than its diff:
```python
import jax
import jax.numpy as jnp
from jax import lax
from jax.experimental import pallas as pl
from jax.experimental.pallas import tpu as pltpu
from jax.sharding import PartitionSpec as P

MESH = pl.DeviceIdType.MESH
BF16 = jnp.bfloat16
F32 = jnp.float32

N = 8
CAP = 40
CHUNK = 48
HID = 128
D = 64 * CHUNK
MAIN = 256
XD = 640
DR = 384


def tn(left, right):
    return lax.dot_general(left, right, (((0,), (0,)), ((), ())), preferred_element_type=F32)


def nt(left, right):
    return lax.dot_general(left, right, (((1,), (1,)), ((), ())), preferred_element_type=F32)


def nn(left, right):
    return lax.dot_general(left, right, (((1,), (0,)), ((), ())), preferred_element_type=F32)


def iota(shape, dim):
    return lax.broadcasted_iota(jnp.int32, shape, dim)


def hops(i, right):
    return 4 if (i % 2 == 0) == right else 3


def kernel(
    x_ref, dy_ref, lang_ref, wg_hbm, wu_hbm, wd_hbm,
    gt_ref, gg_hbm, gu_hbm, gd_hbm,
    wg, wu, wd, wdt, msg, blk, xd, place, oht, acc_gu, acc_d, acc_t, gcat, hcat,
    part, rsend, rrecv, ssend, srecv, bsend, brecv, gg, gu, gd,
    wsem, a_s, a_r, m_s, m_r, g_s, g_r, r_s, r_r, s_s, s_r, b_s, b_r, osem,
):
    e = lax.axis_index("expert")
    hid = lax.axis_index("hidden")
    core = lax.rem(e, 2)
    y, z = hid // N, lax.rem(hid, N)
    a = y * (1 - core) + z * core
    b = z * (1 - core) + y * core
    sa, sb = N - 7 * core, 1 + 7 * core

    def wrap(v):
        return lax.rem(v + 2 * N, N)

    def hx(aa, bb):
        return aa * sa + bb * sb

    def rows(h):
        return pl.ds(pl.multiple_of(h * CHUNK, CHUNK), CHUNK)

    def remote(src, dst, ss, rs, dev):
        return pltpu.make_async_remote_copy(
            src_ref=src, dst_ref=dst, send_sem=ss, recv_sem=rs, device_id=dev, device_id_type=MESH
        )

    bar = pltpu.get_barrier_semaphore()
    for j in range(1, N):
        pl.semaphore_signal(bar, inc=1, device_id={"expert": wrap(e + j)}, device_id_type=MESH)
        pl.semaphore_signal(bar, inc=1, device_id={"hidden": hx(wrap(a + j), b)}, device_id_type=MESH)
    for d in (1, -1):
        pl.semaphore_signal(bar, inc=1, device_id={"hidden": hx(a, wrap(b + d))}, device_id_type=MESH)

    loads = [
        pltpu.make_async_copy(src, dst, wsem.at[k])
        for k, (src, dst) in enumerate(((wg_hbm, wg), (wu_hbm, wu), (wd_hbm, wd)))
    ]
    for c in loads:
        c.start()

    lang = lang_ref[...]
    member = iota((N, 128), 0) == lang
    earlier = (iota((128, 128), 0) < iota((128, 128), 1)).astype(BF16)
    before = nn(member.astype(BF16), earlier)
    slot = jnp.sum(jnp.where(member, before, 0.0), axis=0, keepdims=True).astype(jnp.int32)
    row = lang * 128 + slot
    line = iota((N * 128, 128), 0)
    oht[:, 0:128] = (line == row).astype(BF16)
    oht[:, 128:256] = (line == row + 64).astype(BF16)
    both = jnp.concatenate([x_ref[...], dy_ref[...]], axis=1)
    out = nt(both, oht[...]).astype(BF16)
    for k in range(N):
        msg[k] = out[:, k * 128 : (k + 1) * 128]

    pl.semaphore_wait(bar, 2 * (N - 1) + 2)

    def to_expert(j, src, dst, ss, rs):
        return remote(src.at[wrap(e + j)], dst.at[e], ss.at[j], rs.at[j], {"expert": wrap(e + j)})

    a2a = [to_expert(j, msg, blk, a_s, a_r) for j in range(1, N)]
    for c in a2a:
        c.start()
    blk[e] = msg[e]

    r1 = iota((N * 128, 1), 0)
    blk_i, j_i = r1 // 128, lax.rem(r1, 128)
    is_dy = j_i >= 64
    jj = jnp.where(is_dy, j_i - 64, j_i)
    pos = blk_i * CAP + jj
    lane = jnp.where(
        pos < MAIN, pos + jnp.where(is_dy, MAIN, 0), pos + jnp.where(is_dy, 2 * MAIN - MAIN + 64, 2 * MAIN - MAIN)
    )
    lane = jnp.where(jj < CAP, lane, -1)
    place[...] = (iota((N * 128, XD), 1) == lane).astype(BF16)

    for c in loads:
        c.wait()
    for k in range(D // 128):
        wdt[pl.ds(k * 128, 128), :] = wd[:, k * 128 : (k + 1) * 128].T
    acc_gu[...] = jnp.zeros_like(acc_gu)
    acc_d[...] = jnp.zeros_like(acc_d)
    acc_t[...] = jnp.zeros_like(acc_t)

    for c in a2a:
        c.wait()
    cat = jnp.concatenate([blk[k] for k in range(N)], axis=1)
    xd[hid] = nn(cat, place[...]).astype(BF16)

    def small(k, chunk, to):
        h = hx(wrap(a + chunk), b)
        return remote(xd.at[h], xd.at[h], m_s.at[k], m_r.at[k], {"hidden": hx(wrap(a + to), b)})

    def big(i, off, right, s):
        k, d = (0, 1) if right else (1, -1)
        h = hx(wrap(a + off), wrap(b - d * s))
        return remote(
            xd.at[h], xd.at[h], g_s.at[k, i, s], g_r.at[k, i, s], {"hidden": hx(a, wrap(b + d))}
        )

    def big_recv(i, off, right, s):
        k, d = (0, 1) if right else (1, -1)
        h = hx(wrap(a + off), wrap(b - d * (s + 1)))
        return remote(
            xd.at[h], xd.at[h], g_s.at[k, i, s], g_r.at[k, i, s], {"hidden": hx(a, wrap(b + d))}
        )

    def small_recv(k):
        small(k, k, 0).wait_recv()

    def offset(i2, p):
        return -i2 if p == 0 else i2 + 1

    def send_big(i, off, s, parity=None):
        for right in (True, False):
            if s < hops(i if parity is None else parity, right):
                if s > 0:
                    big_recv(i, off, right, s - 1).wait_recv()
                big(i, off, right, s).start()

    even = lax.rem(a, 2)
    far = 2 - 4 * even
    sends = [small(1, 0, -1), small(7, 0, 1), small(2, 0, -2), small(6, 0, 2)]
    sends[0].start()
    sends[1].start()
    send_big(0, 0, 0)
    sends[2].start()
    sends[3].start()
    small_recv(1)
    send_big(1, 1, 0)
    small_recv(7)
    send_big(2, -1, 0)
    small_recv(2)
    relay = [small(3, 2, -1), small(5, -2, 1), small(4, far, -far)]
    relay[0].start()
    small_recv(6)
    relay[1].start()
    relay[2].start()
    send_big(3, 2, 0)
    send_big(4, -2, 0)
    send_big(0, 0, 1)
    small_recv(3)
    send_big(5, 3, 0)
    small_recv(5)
    send_big(6, -3, 0)
    small_recv(4)
    send_big(7, 4, 0)

    def column(ref, dist):
        o = wrap(b + dist)
        return [hx(wrap(a + r), o) for r in range(N)]

    def forward(dist):
        hs = column(xd, dist)
        left = jnp.concatenate(
            [jnp.concatenate([wg[rows(h), :], wu[rows(h), :], wdt[rows(h), :]], axis=1) for h in hs], axis=0
        )
        right = jnp.concatenate([xd[h] for h in hs], axis=0)
        acc_gu[...] += tn(left[:, 0 : 2 * HID], right[:, 0:MAIN])
        acc_d[...] += tn(left[:, 2 * HID : 3 * HID], right[:, MAIN : 2 * MAIN])
        acc_t[...] += tn(left, right[:, 2 * MAIN : XD])

    forward(0)
    for s in range(1, 4):
        def step(i2, carry):
            for p in (0, 1):
                send_big(2 * i2 + p, offset(i2, p), s, p)
            return carry

        if s == 1:
            send_big(1, 1, 1)
            lax.fori_loop(1, 4, step, 0)
        else:
            lax.fori_loop(0, 4, step, 0)

        if s == 3:
            def last(i2, carry):
                for p in (0, 1):
                    for right in (True, False):
                        if hops(p, right) == 3:
                            big_recv(2 * i2 + p, offset(i2, p), right, 2).wait_recv()
                return carry

            lax.fori_loop(0, 4, last, 0)

        def two(k, carry):
            forward((1 - 2 * k) * s)
            return carry

        lax.fori_loop(0, 2, two, 0)

    def end(i2, carry):
        for p in (0, 1):
            for right in (True, False):
                if hops(p, right) == 4:
                    big_recv(2 * i2 + p, offset(i2, p), right, 3).wait_recv()
        return carry

    lax.fori_loop(0, 4, end, 0)
    forward(4)

    def units(gate, up, dh):
        sig = jax.nn.sigmoid(gate)
        act = gate * sig
        return (
            (act * up).astype(BF16),
            (dh * up * sig * (1.0 + gate * (1.0 - sig))).astype(BF16),
            (dh * act).astype(BF16),
        )

    h_m, g_m, u_m = units(acc_gu[0:HID, :], acc_gu[HID : 2 * HID, :], acc_d[...])
    tail = acc_t[...]
    dh_t = pltpu.roll(tail[2 * HID : 3 * HID, :], 64, 1)
    h_t, g_t, u_t = units(tail[0:HID, :], tail[HID : 2 * HID, :], dh_t)
    low = iota((HID, 128), 1) < 64
    zero = jnp.zeros((HID, 128), BF16)
    gcat[0:HID, 0:MAIN] = g_m
    gcat[HID : 2 * HID, 0:MAIN] = u_m
    gcat[0:HID, MAIN:DR] = jnp.where(low, g_t, zero)
    gcat[HID : 2 * HID, MAIN:DR] = jnp.where(low, u_t, zero)
    hcat[:, 0:MAIN] = h_m
    h_shift = pltpu.roll(h_t.astype(F32), 64, 1).astype(BF16)
    hcat[:, MAIN:DR] = jnp.where(low, zero, h_shift)

    def partial_sums(dist):
        hs = column(part, dist)
        left = jnp.concatenate(
            [jnp.concatenate([wg[rows(h), :], wu[rows(h), :]], axis=1) for h in hs], axis=0
        )
        part[dist % N] = nn(left, gcat[...]).reshape(N, CHUNK, DR)

    def reduce_copy(i, right, s):
        k, d = (0, 1) if right else (1, -1)
        return remote(
            rsend.at[k, i, s], rrecv.at[k, i, s], r_s.at[k, i, s], r_r.at[k, i, s], {"hidden": hx(a, wrap(b + d))}
        )

    def reduce_step(i, p, right, s):
        k, d = (0, 1) if right else (1, -1)
        far_off = d * (hops(p, right) - s)
        value = part[far_off % N, i]
        if s > 0:
            reduce_copy(i, right, s - 1).wait_recv()
            value = value + rrecv[k, i, s - 1].astype(F32)
        rsend[k, i, s] = value.astype(BF16)
        reduce_copy(i, right, s).start()

    def reduce_stage(s, pick):
        def step(i2, carry):
            for p in (0, 1):
                for right in (True, False):
                    if s < hops(p, right) and hops(p, right) in pick:
                        reduce_step(2 * i2 + p, p, right, s)
            return carry

        lax.fori_loop(0, 4, step, 0)

    outs = []

    def weight_grads(g):
        first = g * N * CHUNK
        span = pl.ds(pl.multiple_of(first, N * CHUNK), N * CHUNK)
        feat = xd[pl.ds(g * N, N)].reshape(N * CHUNK, XD)
        x_rows = jnp.concatenate([feat[:, 0:MAIN], feat[:, 2 * MAIN : XD]], axis=1)
        dy_rows = feat[:, MAIN:XD]
        pair = nt(x_rows, gcat[...]).astype(BF16)
        gg[span, :] = pair[:, 0:HID]
        gu[span, :] = pair[:, HID : 2 * HID]
        gd[:, span] = nt(hcat[...], dy_rows).astype(BF16)
        for k, (src, dst) in enumerate(((gg, gg_hbm), (gu, gu_hbm))):
            pltpu.make_async_copy(src.at[span, :], dst.at[span, :], osem.at[k, g]).start()
        pltpu.make_async_copy(gd.at[:, span], gd_hbm.at[:, span], osem.at[2, g]).start()

    def grads(lo, hi):
        def one(g, carry):
            weight_grads(g)
            return carry

        lax.fori_loop(lo, hi, one, 0)

    partial_sums(4)
    reduce_stage(0, (4,))
    partial_sums(3)
    partial_sums(-3)
    reduce_stage(0, (3,))
    for dist in (2, -2, 1, -1, 0):
        partial_sums(dist)
    reduce_stage(1, (3, 4))
    grads(0, 2)
    reduce_stage(2, (3, 4))
    grads(2, 5)
    reduce_stage(3, (3, 4))
    grads(5, 8)

    def collect(i, p):
        value = part[0, i]
        for right in (True, False):
            k, s = (0 if right else 1), hops(p, right) - 1
            reduce_copy(i, right, s).wait_recv()
            value = value + rrecv[k, i, s].astype(F32)
        return value

    def small_sum(i):
        return remote(
            ssend.at[i], srecv.at[i], s_s.at[i], s_r.at[i], {"hidden": hx(wrap(a + i), b)}
        )

    for i in (4, 3, 5, 2, 6, 1, 7):
        ssend[i] = collect(i, i % 2).astype(BF16)
        small_sum(i).start()
    total = collect(0, 0)

    p_i = iota((DR, N * 128), 0)
    c_i = iota((DR, N * 128), 1)
    j_c = lax.rem(c_i, 128)
    pick = ((p_i == (c_i // 128) * CAP + j_c) & (j_c < CAP)).astype(BF16)

    for i in (1, 7, 2, 6, 3, 5, 4):
        small_sum(i).wait_recv()
        total = total + srecv[i].astype(F32)
    back = nn(total.astype(BF16), pick).astype(BF16)
    for k in range(N):
        bsend[k] = back[:, k * 128 : (k + 1) * 128]
    home = [to_expert(j, bsend, brecv, b_s, b_r) for j in range(1, N)]
    for c in home:
        c.start()
    brecv[e] = bsend[e]

    for c in sends + relay:
        c.wait_send()

    def close(i2, carry):
        for p in (0, 1):
            for right in (True, False):
                for s in range(hops(p, right)):
                    big(2 * i2 + p, offset(i2, p), right, s).wait_send()
                    reduce_copy(2 * i2 + p, right, s).wait_send()
        return carry

    lax.fori_loop(0, 4, close, 0)
    for i in range(1, N):
        small_sum(i).wait_send()

    def flush(g, carry):
        span = pl.ds(pl.multiple_of(g * N * CHUNK, N * CHUNK), N * CHUNK)
        for k, (src, dst) in enumerate(((gg, gg_hbm), (gu, gu_hbm))):
            pltpu.make_async_copy(src.at[span, :], dst.at[span, :], osem.at[k, g]).wait()
        pltpu.make_async_copy(gd.at[:, span], gd_hbm.at[:, span], osem.at[2, g]).wait()
        return carry

    lax.fori_loop(0, N, flush, 0)

    for c in home:
        c.wait()
    cat = jnp.concatenate([brecv[k] for k in range(N)], axis=1)
    gt_ref[...] = nn(cat, oht[:, 0:128]).astype(BF16)


def local(tokens, grad_out, lang_ids, gate_weight, up_weight, down_weight):
    vmem = pl.BlockSpec(memory_space=pltpu.VMEM)
    anyspace = pl.BlockSpec(memory_space=pl.ANY)
    dma = pltpu.SemaphoreType.DMA
    scratch = [
        pltpu.VMEM((D, HID), BF16),
        pltpu.VMEM((D, HID), BF16),
        pltpu.VMEM((HID, D), BF16),
        pltpu.VMEM((D, HID), BF16),
        pltpu.VMEM((N, CHUNK, 128), BF16),
        pltpu.VMEM((N, CHUNK, 128), BF16),
        pltpu.VMEM((64, CHUNK, XD), BF16),
        pltpu.VMEM((N * 128, XD), BF16),
        pltpu.VMEM((N * 128, 256), BF16),
        pltpu.VMEM((2 * HID, MAIN), F32),
        pltpu.VMEM((HID, MAIN), F32),
        pltpu.VMEM((3 * HID, 128), F32),
        pltpu.VMEM((2 * HID, DR), BF16),
        pltpu.VMEM((HID, DR), BF16),
        pltpu.VMEM((N, N, CHUNK, DR), F32),
        pltpu.VMEM((2, N, 4, CHUNK, DR), BF16),
        pltpu.VMEM((2, N, 4, CHUNK, DR), BF16),
        pltpu.VMEM((N, CHUNK, DR), BF16),
        pltpu.VMEM((N, CHUNK, DR), BF16),
        pltpu.VMEM((N, CHUNK, 128), BF16),
        pltpu.VMEM((N, CHUNK, 128), BF16),
        pltpu.VMEM((D, HID), BF16),
        pltpu.VMEM((D, HID), BF16),
        pltpu.VMEM((HID, D), BF16),
        dma((3,)),
        dma((N,)), dma((N,)),
        dma((N,)), dma((N,)),
        dma((2, N, 4)), dma((2, N, 4)),
        dma((2, N, 4)), dma((2, N, 4)),
        dma((N,)), dma((N,)),
        dma((N,)), dma((N,)),
        dma((3, N)),
    ]
    out = pl.pallas_call(
        kernel,
        out_shape=(
            jax.ShapeDtypeStruct((CHUNK, 128), BF16),
            jax.ShapeDtypeStruct((D, HID), BF16),
            jax.ShapeDtypeStruct((D, HID), BF16),
            jax.ShapeDtypeStruct((HID, D), BF16),
        ),
        in_specs=[vmem, vmem, vmem, anyspace, anyspace, anyspace],
        out_specs=(vmem, anyspace, anyspace, anyspace),
        scratch_shapes=scratch,
        compiler_params=pltpu.CompilerParams(
            collective_id=0, has_side_effects=True, vmem_limit_bytes=56 * 1024 * 1024
        ),
        cost_estimate=pl.CostEstimate(
            flops=16 * 320 * D * HID, bytes_accessed=6 * D * HID * 2, transcendentals=320 * HID
        ),
    )(
        tokens.T, grad_out.T, lang_ids.T, gate_weight[0], up_weight[0], down_weight[0]
    )
    return out[0].T, out[1][None], out[2][None], out[3][None]


def solution(mesh):
    in_specs = (
        P("expert", "hidden"),
        P("expert", "hidden"),
        P("expert", None),
        P("expert", None, "hidden"),
        P("expert", None, "hidden"),
        P("expert", "hidden", None),
    )
    out_specs = (
        P("expert", "hidden"),
        P("expert", None, "hidden"),
        P("expert", None, "hidden"),
        P("expert", "hidden", None),
    )
    return jax.shard_map(local, mesh=mesh, in_specs=in_specs, out_specs=out_specs, check_vma=False)
```

time: 575 us -> 89.2 us (0.16)
  blocking collectives: 293 us -> 0 us
  waiting for transfers between devices: 155 us -> 0 us
  Pallas kernels: 0 us -> 82.5 us
  starting transfers between devices: 59.4 us -> 0 us
  local copies, waits for them, and re-layouts: 36.8 us -> 5.73 us
  between operations: 14.8 us -> 0.65 us
  matrix products: 13.4 us -> 0 us
    unnamed x1 -> x0, blocking collectives: 271 us -> none
    all_gather x2 -> x0, waiting for transfers between devices: 152 us -> none  [the longest x1 81.4 us: local(): lax.all_gather(dy_blocks, 'hidden', axis=2, tiled=True)]
    pallas_call x0 -> x1, Pallas kernels: none -> 82.5 us  [local(): pl.pallas_call(kernel, out_shape=(jax.ShapeDtypeStruct((CHUNK, 128), BF16...]
    all_to_all x1 -> x0, starting transfers between devices: 59.3 us -> none  [local(): lax.all_to_all(summed.astype(jnp.bfloat16), 'expert', split_axis=0, conca...]
    all_to_all x2 -> x0, blocking collectives: 21.8 us -> none  [the longest x1 14 us: local(): lax.all_to_all(place(tokens), 'expert', split_axis=0, concat_axis=0, tile...]
    scatter x2 -> x0, local copies, waits for them, and re-layouts: 14.2 us -> none  [place(): return empty.at[expert_ids, slots].set(values)]
    all_gather x2 -> x0, local copies, waits for them, and re-layouts: 13.8 us -> none  [the longest x1 7.42 us: local(): lax.all_gather(dy_blocks, 'hidden', axis=2, tiled=True)]
    dot_general x8 -> x0, matrix products: 13.4 us -> none  [the longest x3 6.83 us: contract_rows(): lax.dot_general(left, right, (((0,), (0,)), ((), ())), preferred_element_...]
  transfers between devices with their start and end apart: 3 -> 0, of which waited for: 3 -> 0; matrix products, arithmetic and copies ran while one was open for 4% -> 0% of each run, Pallas kernels for 0% -> 0%
where the time goes in v1:
time: 89.2 us; the launch traced here: 88.9 us
  Pallas kernels  82.5 us (92%)
  local copies, waits for them, and re-layouts  5.73 us (6%)
    pallas_call x1, Pallas kernels, local(): pl.pallas_call(kernel, out_shape=(jax.ShapeDtypeStruct((CHUNK, 128), BF16...  82.5 us
    unnamed x10, local copies, waits for them, and re-layouts  5.73 us

profile of v1, /device:TPU:1, one launch (start us, length us, event | category | flops | bytes accessed | tf_op | source)
XLA Modules:
  0.0 88.9 jit_solution(10265165296011966346)
XLA Ops:
  0.6 82.5 %shard_map.93 = (bf16[48,128]{1,0:T(8,128)(2,1)}, bf16[3072,128]{1,0:T(8,128)(2,1)}, bf16[3072,128]{1,0:T(8,128)(2,1)}, bf16[128,3072]{1,0:T(8,128)(2,1)}) custom-call(bf16[48,128]{1,0:T(8,128)(2,1)} %bitcast.17, bf16[48,128]{1,0:T(8,128)(2,1)} %bitcast.18, s32[1,128]{1,0:T(1,128)} %bitcast.19, bf16[3072,128]{1,0:T(8,128)(2,1)} %bitcast.14, ...), custom_call_target="tpu_custom_call" | custom-call | flops 2013265920 | bytes 4718592 | tf_op jit(solution)/shard_map/pallas_call | solution.py:440
  83.2 0.0 copy-start.2
  83.2 0.7 copy-done.2
  83.9 0.6 copy.14
  84.5 0.0 copy-start.1
  84.5 2.1 %copy.15 = bf16[1,3072,128]{2,1,0:T(8,128)(2,1)} copy(bf16[1,3072,128]{2,1,0:T(8,128)(2,1)} %bitcast.12) | data formatting | bytes 1572864
  86.6 0.0 copy-done.1
  86.6 0.0 copy-start
  86.6 0.9 copy.16
  87.5 0.5 copy-done
  88.0 0.9 copy.17
Async XLA Ops:
  83.2 0.7 copy-start.2
  84.5 2.1 %copy-start.1 = (bf16[3072,128]{1,0:T(8,128)(2,1)S(1)}, bf16[3072,128]{1,0:T(8,128)(2,1)}, u32[]{:S(2)}) copy-start(bf16[3072,128]{1,0:T(8,128)(2,1)} %get-tuple-element.10) | copy-start | bytes 2359300
  86.6 1.4 %copy-start = (bf16[128,3072]{1,0:T(8,128)(2,1)S(1)}, bf16[128,3072]{1,0:T(8,128)(2,1)}, u32[]{:S(2)}) copy-start(bf16[128,3072]{1,0:T(8,128)(2,1)} %get-tuple-element.11) | copy-start | bytes 2359300

commit v2 on v1

v2 whole, which is shorter than its diff:
```python
import jax
import jax.numpy as jnp
from jax import lax
from jax.experimental import pallas as pl
from jax.experimental.pallas import tpu as pltpu
from jax.sharding import PartitionSpec as P

MESH = pl.DeviceIdType.MESH
BF16 = jnp.bfloat16
F32 = jnp.float32

N = 8
CAP = 40
CHUNK = 48
HID = 128
D = 64 * CHUNK
MAIN = 256
XD = 640
DR = 384


def tn(left, right):
    return lax.dot_general(left, right, (((0,), (0,)), ((), ())), preferred_element_type=F32)


def nt(left, right):
    return lax.dot_general(left, right, (((1,), (1,)), ((), ())), preferred_element_type=F32)


def nn(left, right):
    return lax.dot_general(left, right, (((1,), (0,)), ((), ())), preferred_element_type=F32)


def iota(shape, dim):
    return lax.broadcasted_iota(jnp.int32, shape, dim)


def off(i, odd):
    return 2 * i - 4 + odd


ORDER = (2, 1, 3, 0)
PEERS = (4, 3, 5, 2, 6, 1, 7)


def kernel(
    x_hbm, dy_hbm, lang_hbm, wg_hbm, wu_hbm, wd_hbm,
    gt_ref, gg_hbm, gu_hbm, gd_hbm,
    x_ref, dy_ref, lang_ref, wg, wu, wd, wdt, msg, blk, xd, place, oht, acc_gu, acc_d, acc_t, gcat, hcat,
    part, rsend, rrecv, ssend, srecv, bsend, brecv, gg, gu, gd,
    tsem, wsem, a_s, a_r, m_s, m_r, g_s, g_r, r_s, r_r, s_s, s_r, b_s, b_r, osem,
):
    tok = [
        pltpu.make_async_copy(src, dst, tsem.at[k])
        for k, (src, dst) in enumerate(((lang_hbm, lang_ref), (x_hbm, x_ref), (dy_hbm, dy_ref)))
    ]
    for c in tok:
        c.start()

    e = lax.axis_index("expert")
    hid = lax.axis_index("hidden")
    core = lax.rem(e, 2)
    y, z = hid // N, lax.rem(hid, N)
    own = lax.rem(y + z + core, 2)
    way = (own, 1 - own)

    def wrap(v):
        return lax.rem(v + 2 * N, N)

    def way_of(q):
        return lax.rem(own + q, 2)

    def first(q):
        c = way_of(q)
        return y * (1 - c) + z * c

    def hx(q, du, dv):
        c = way_of(q)
        u = wrap(y * (1 - c) + z * c + du)
        v = wrap(z * (1 - c) + y * c + dv)
        return u * (N - 7 * c) + v * (1 + 7 * c)

    def side(q, odd):
        return lax.rem((first(q) + odd) // 2, 2)

    def rows(h):
        return pl.ds(pl.multiple_of(h * CHUNK, CHUNK), CHUNK)

    def remote(src, dst, ss, rs, dev):
        return pltpu.make_async_remote_copy(
            src_ref=src, dst_ref=dst, send_sem=ss, recv_sem=rs, device_id=dev, device_id_type=MESH
        )

    bar = pltpu.get_barrier_semaphore()
    for j in range(1, N):
        pl.semaphore_signal(bar, inc=1, device_id={"expert": wrap(e + j)}, device_id_type=MESH)
        pl.semaphore_signal(bar, inc=1, device_id={"hidden": hx(0, j, 0)}, device_id_type=MESH)
    for j in (1, -1, 3, -3):
        pl.semaphore_signal(bar, inc=1, device_id={"hidden": hx(1, j, 0)}, device_id_type=MESH)

    loads = [
        pltpu.make_async_copy(src, dst, wsem.at[k])
        for k, (src, dst) in enumerate(((wg_hbm, wg), (wu_hbm, wu), (wd_hbm, wd)))
    ]
    for c in loads:
        c.start()
    for c in tok:
        c.wait()

    lang = lang_ref[...]
    member = iota((N, 128), 0) == lang
    earlier = (iota((128, 128), 0) < iota((128, 128), 1)).astype(BF16)
    before = nn(member.astype(BF16), earlier)
    slot = jnp.sum(jnp.where(member, before, 0.0), axis=0, keepdims=True).astype(jnp.int32)
    oht[...] = (iota((N * 64, 128), 0) == lang * 64 + slot).astype(BF16)
    out = nt(jnp.concatenate([x_ref[...], dy_ref[...]], axis=0), oht[...])
    low = iota((CHUNK, 128), 1) < 64
    for k in range(N):
        tile = slice(k // 2 * 128, k // 2 * 128 + 128)
        x_k, dy_k = out[0:CHUNK, tile], out[CHUNK : 2 * CHUNK, tile]
        if k % 2 == 0:
            dy_k = pltpu.roll(dy_k, 64, 1)
        else:
            x_k = pltpu.roll(x_k, 64, 1)
        msg[k] = jnp.where(low, x_k, dy_k).astype(BF16)

    pl.semaphore_wait(bar, 2 * (N - 1) + 4)

    def to_expert(j, src, dst, ss, rs):
        return remote(src.at[wrap(e + j)], dst.at[e], ss.at[j], rs.at[j], {"expert": wrap(e + j)})

    a2a = [to_expert(j, msg, blk, a_s, a_r) for j in PEERS]
    for c in a2a:
        c.start()
    blk[e] = msg[e]

    r1 = iota((N * 128, 1), 0)
    blk_i, j_i = r1 // 128, lax.rem(r1, 128)
    is_dy = j_i >= 64
    jj = jnp.where(is_dy, j_i - 64, j_i)
    pos = blk_i * CAP + jj
    lane = jnp.where(pos < MAIN, pos + jnp.where(is_dy, MAIN, 0), pos + jnp.where(is_dy, MAIN + 64, MAIN))
    lane = jnp.where(jj < CAP, lane, -1)
    place[...] = (iota((N * 128, XD), 1) == lane).astype(BF16)

    for c in loads:
        c.wait()
    for k in range(D // 128):
        wdt[pl.ds(k * 128, 128), :] = wd[:, k * 128 : (k + 1) * 128].T
    acc_gu[...] = jnp.zeros_like(acc_gu)
    acc_d[...] = jnp.zeros_like(acc_d)
    acc_t[...] = jnp.zeros_like(acc_t)

    for c in a2a:
        c.wait()
    cat = jnp.concatenate([blk[k] for k in range(N)], axis=1)
    xd[hid] = nn(cat, place[...]).astype(BF16)

    def small(k, q, chunk, to):
        h = hx(q, chunk, 0)
        return remote(xd.at[h], xd.at[h], m_s.at[k], m_r.at[k], {"hidden": hx(q, to, 0)})

    def small_recv(k):
        h = hx(k % 2, k, 0)
        remote(xd.at[h], xd.at[h], m_s.at[k], m_r.at[k], {"hidden": hid}).wait_recv()

    def big(q, i, d, s):
        to = 1 - 2 * d
        h = hx(q, off(i, (s + q) % 2), -to * s)
        c = way[q]
        return remote(
            xd.at[h], xd.at[h], g_s.at[c, d, s, i], g_r.at[c, d, s, i], {"hidden": hx(q, 0, to)}
        )

    def big_recv(q, i, d, s):
        to = 1 - 2 * d
        h = hx(q, off(i, (s + 1 + q) % 2), -to * (s + 1))
        c = way[q]
        remote(xd.at[h], xd.at[h], g_s.at[c, d, s, i], g_r.at[c, d, s, i], {"hidden": hid}).wait_recv()

    def goes_far(q, d, s):
        c = side(q, (s + q) % 2)
        c = c if d == 0 else 1 - c
        return [c, c + 2]

    def stays(q, d, s):
        c = side(q, (s + q) % 2)
        c = 1 - c if d == 0 else c
        return [c, c + 2]

    def send_big(q, i, s):
        for d in (0, 1):
            if s > 0:
                big_recv(q, i, d, s - 1)
            big(q, i, d, s).start()

    turn = side(0, 0)
    far = 2 - 4 * turn
    sends = [small(1, 0, 0, -1), small(7, 0, 0, 1), small(2, 0, 0, -2), small(6, 0, 0, 2)]
    relay = [small(3, 0, 2, -1), small(5, 0, -2, 1), small(4, 0, far, -far)]
    sends[0].start()
    sends[1].start()
    send_big(0, 2, 0)
    sends[2].start()
    sends[3].start()
    small_recv(1)
    send_big(1, 2, 0)
    small_recv(7)
    send_big(1, 1, 0)
    small_recv(2)
    relay[0].start()
    small_recv(6)
    relay[1].start()
    relay[2].start()
    send_big(0, 3, 0)
    send_big(0, 1, 0)
    send_big(1, 2, 1)
    small_recv(3)
    send_big(1, 3, 0)
    small_recv(5)
    send_big(1, 0, 0)
    small_recv(4)
    send_big(0, 0, 0)

    def forward(hs):
        left = jnp.concatenate(
            [jnp.concatenate([wg[rows(h), :], wu[rows(h), :], wdt[rows(h), :]], axis=1) for h in hs], axis=0
        )
        right = jnp.concatenate([xd[h] for h in hs], axis=0)
        acc_gu[...] += tn(left[:, 0 : 2 * HID], right[:, 0:MAIN])
        acc_d[...] += tn(left[:, 2 * HID : 3 * HID], right[:, MAIN : 2 * MAIN])
        acc_t[...] += tn(left, right[:, 2 * MAIN : XD])

    def column(dist):
        return [hx(q, off(i, (q + dist) % 2), dist) for q in (0, 1) for i in range(4)]

    forward(column(0))
    for s in range(1, 4):
        if s < 3:
            for i in ORDER:
                for q in (0, 1):
                    if (s, q, i) != (1, 1, 2):
                        send_big(q, i, s)
        else:
            for j in (0, 1):
                for q in (0, 1):
                    for d in (0, 1):
                        i = goes_far(q, d, 3)[j]
                        big_recv(q, i, d, 2)
                        big(q, i, d, 3).start()
            for q in (0, 1):
                for d in (0, 1):
                    for i in stays(q, d, 3):
                        big_recv(q, i, d, 2)

        def two(k, carry):
            forward(column((1 - 2 * k) * s))
            return carry

        lax.fori_loop(0, 2, two, 0)

    for q in (0, 1):
        for d in (0, 1):
            for i in goes_far(q, d, 4):
                big_recv(q, i, d, 3)
    forward(column(4))

    def units(gate, up, dh):
        sig = jax.nn.sigmoid(gate)
        act = gate * sig
        return (
            (act * up).astype(BF16),
            (dh * up * sig * (1.0 + gate * (1.0 - sig))).astype(BF16),
            (dh * act).astype(BF16),
        )

    h_m, g_m, u_m = units(acc_gu[0:HID, :], acc_gu[HID : 2 * HID, :], acc_d[...])
    tail = acc_t[...]
    dh_t = pltpu.roll(tail[2 * HID : 3 * HID, :], 64, 1)
    h_t, g_t, u_t = units(tail[0:HID, :], tail[HID : 2 * HID, :], dh_t)
    low_h = iota((HID, 128), 1) < 64
    for k, (m, t) in enumerate(((g_m, g_t), (u_m, u_t))):
        span = slice(k * HID, (k + 1) * HID)
        t = jnp.where(low_h, t.astype(F32), 0.0)
        gcat[span, 0:MAIN] = m
        gcat[span, MAIN:DR] = t.astype(BF16)
        gcat[span, DR : DR + 128] = pltpu.roll(t, 64, 1).astype(BF16)
    hcat[:, 0:MAIN] = h_m
    hcat[:, MAIN:DR] = pltpu.roll(jnp.where(low_h, h_t.astype(F32), 0.0), 64, 1).astype(BF16)

    def partial_sums(dist):
        hs = column(dist)
        left = jnp.concatenate(
            [jnp.concatenate([wg[rows(h), :], wu[rows(h), :]], axis=1) for h in hs], axis=0
        )
        res = nn(left, gcat[...])
        for n, h in enumerate(hs):
            block = res[n * CHUNK : (n + 1) * CHUNK]
            part[h, :, 0:MAIN] = block[:, 0:MAIN]
            part[h, :, MAIN:DR] = block[:, MAIN:DR] if n % 4 < 2 else block[:, DR : DR + 128]

    def reduce_copy(q, d, short, s):
        c = way[q]
        return remote(
            rsend.at[c, d, short, s],
            rrecv.at[c, d, short, s],
            r_s.at[c, d, short, s],
            r_r.at[c, d, short, s],
            {"hidden": hx(q, 0, 1 - 2 * d)},
        )

    def pair_parts(q, sel, odd, dist):
        h0, h1 = hx(q, off(sel, odd), dist), hx(q, off(sel + 2, odd), dist)
        return [part[h0, :, 0:MAIN], part[h1, :, 0:MAIN], part[h0, :, MAIN:DR] + part[h1, :, MAIN:DR]]

    def add_message(values, message):
        spans = ((0, MAIN), (MAIN, 2 * MAIN), (2 * MAIN, XD))
        return [v + message[:, lo:hi].astype(F32) for v, (lo, hi) in zip(values, spans)]

    def reduce_step(q, d, short, s):
        left_hops = 4 - short - s
        odd = (q + left_hops) % 2
        sel = side(q, odd)
        sel = sel if d == short else 1 - sel
        values = pair_parts(q, sel, odd, (1 - 2 * d) * left_hops)
        c = way[q]
        if s > 0:
            reduce_copy(q, d, short, s - 1).wait_recv()
            values = add_message(values, rrecv[c, d, short, s - 1])
        rsend[c, d, short, s] = jnp.concatenate([v.astype(BF16) for v in values], axis=1)
        reduce_copy(q, d, short, s).start()

    def reduce_stage(s, pick):
        for short in pick:
            for q in (0, 1):
                for d in (0, 1):
                    reduce_step(q, d, short, s)

    def weight_grads(g):
        span = pl.ds(pl.multiple_of(g * N * CHUNK, N * CHUNK), N * CHUNK)
        feat = xd[pl.ds(g * N, N)].reshape(N * CHUNK, XD)
        x_rows = jnp.concatenate([feat[:, 0:MAIN], feat[:, 2 * MAIN : XD]], axis=1)
        dy_rows = feat[:, MAIN:XD]
        pair = nt(x_rows, gcat[:, 0:DR]).astype(BF16)
        gg[span, :] = pair[:, 0:HID]
        gu[span, :] = pair[:, HID : 2 * HID]
        gd[:, span] = nt(hcat[...], dy_rows).astype(BF16)
        for k, (src, dst) in enumerate(((gg, gg_hbm), (gu, gu_hbm))):
            pltpu.make_async_copy(src.at[span, :], dst.at[span, :], osem.at[k, g]).start()
        pltpu.make_async_copy(gd.at[:, span], gd_hbm.at[:, span], osem.at[2, g]).start()

    def grads(lo, hi):
        def one(g, carry):
            weight_grads(g)
            return carry

        lax.fori_loop(lo, hi, one, 0)

    partial_sums(4)
    reduce_stage(0, (0,))
    partial_sums(3)
    partial_sums(-3)
    reduce_stage(0, (1,))

    def rest(k, carry):
        partial_sums(k - 2)
        return carry

    lax.fori_loop(0, 5, rest, 0)
    reduce_stage(1, (0, 1))
    grads(0, 3)
    reduce_stage(2, (0, 1))
    grads(3, 6)
    reduce_stage(3, (0,))
    grads(6, 8)

    def small_sum(k, q):
        return remote(ssend.at[k], srecv.at[k], s_s.at[k], s_r.at[k], {"hidden": hx(q, k, 0)})

    for q, sel in ((1, 0), (1, 1), (0, 1), (0, 0)):
        bit = lax.rem(side(q, q) + sel, 2)
        c = way[q]
        values = pair_parts(q, sel, q, 0)
        for d, short in ((0, bit), (1, 1 - bit)):
            last = 3 - short
            remote(
                rsend.at[c, d, short, last],
                rrecv.at[c, d, short, last],
                r_s.at[c, d, short, last],
                r_r.at[c, d, short, last],
                {"hidden": hid},
            ).wait_recv()
            values = add_message(values, rrecv[c, d, short, last])
        for j in (0, 1):
            k = off(sel + 2 * j, q) % N
            if k == 0:
                main, high = values[1], values[2]
            else:
                ssend[k] = jnp.concatenate([values[j].astype(BF16), values[2].astype(BF16)], axis=1)
                small_sum(k, q).start()
    low_sum = jnp.zeros((CHUNK, 128), F32)

    p_i = iota((DR, N * 128), 0)
    c_i = iota((DR, N * 128), 1)
    j_c = lax.rem(c_i, 128) - 64 * core
    pick = ((p_i == (c_i // 128) * CAP + j_c) & (j_c >= 0) & (j_c < CAP)).astype(BF16)

    for k in (1, 7, 2, 6, 3, 5, 4):
        remote(ssend.at[k], srecv.at[k], s_s.at[k], s_r.at[k], {"hidden": hid}).wait_recv()
        main = main + srecv[k, :, 0:MAIN].astype(F32)
        if k >= 4:
            low_sum = low_sum + srecv[k, :, MAIN:DR].astype(F32)
        else:
            high = high + srecv[k, :, MAIN:DR].astype(F32)
    tail = low_sum + pltpu.roll(high, 64, 1)
    total = jnp.concatenate([main.astype(BF16), tail.astype(BF16)], axis=1)
    back = nn(total, pick).astype(BF16)
    for k in range(N):
        bsend[k] = back[:, k * 128 : (k + 1) * 128]
    home = [to_expert(j, bsend, brecv, b_s, b_r) for j in PEERS]
    for c in home:
        c.start()
    brecv[e] = bsend[e]

    for c in sends + relay:
        c.wait_send()
    for q in (0, 1):
        for d in (0, 1):
            for s in range(3):
                for i in range(4):
                    big(q, i, d, s).wait_send()
            for i in goes_far(q, d, 3):
                big(q, i, d, 3).wait_send()
            for short in (0, 1):
                for s in range(4 - short):
                    reduce_copy(q, d, short, s).wait_send()
    for k in range(1, N):
        small_sum(k, k % 2).wait_send()

    def flush(g, carry):
        span = pl.ds(pl.multiple_of(g * N * CHUNK, N * CHUNK), N * CHUNK)
        for k, (src, dst) in enumerate(((gg, gg_hbm), (gu, gu_hbm))):
            pltpu.make_async_copy(src.at[span, :], dst.at[span, :], osem.at[k, g]).wait()
        pltpu.make_async_copy(gd.at[:, span], gd_hbm.at[:, span], osem.at[2, g]).wait()
        return carry

    lax.fori_loop(0, N, flush, 0)

    for c in home:
        c.wait()
    cat = jnp.concatenate([jnp.where(low, brecv[k], brecv[k + 1]) for k in range(0, N, 2)], axis=1)
    gt_ref[...] = nn(cat, oht[...]).astype(BF16)


def copy_kernel(gt, gg, gu, gd, gt_out, gg_out, gu_out, gd_out, sem):
    copies = [
        pltpu.make_async_copy(src, dst, sem.at[k])
        for k, (src, dst) in enumerate(((gg, gg_out), (gu, gu_out), (gd, gd_out)))
    ]
    for c in copies:
        c.start()
    gt_out[...] = gt[...]
    for c in copies:
        c.wait()


def local(tokens, grad_out, lang_ids, gate_weight, up_weight, down_weight):
    vmem = pl.BlockSpec(memory_space=pltpu.VMEM)
    anyspace = pl.BlockSpec(memory_space=pl.ANY)
    hbm = pl.BlockSpec(memory_space=pltpu.HBM)
    dma = pltpu.SemaphoreType.DMA
    scratch = [
        pltpu.VMEM((CHUNK, 128), BF16),
        pltpu.VMEM((CHUNK, 128), BF16),
        pltpu.VMEM((1, 128), jnp.int32),
        pltpu.VMEM((D, HID), BF16),
        pltpu.VMEM((D, HID), BF16),
        pltpu.VMEM((HID, D), BF16),
        pltpu.VMEM((D, HID), BF16),
        pltpu.VMEM((N, CHUNK, 128), BF16),
        pltpu.VMEM((N, CHUNK, 128), BF16),
        pltpu.VMEM((64, CHUNK, XD), BF16),
        pltpu.VMEM((N * 128, XD), BF16),
        pltpu.VMEM((N * 64, 128), BF16),
        pltpu.VMEM((2 * HID, MAIN), F32),
        pltpu.VMEM((HID, MAIN), F32),
        pltpu.VMEM((3 * HID, 128), F32),
        pltpu.VMEM((2 * HID, DR + 128), BF16),
        pltpu.VMEM((HID, DR), BF16),
        pltpu.VMEM((64, CHUNK, DR), F32),
        pltpu.VMEM((2, 2, 2, 4, CHUNK, XD), BF16),
        pltpu.VMEM((2, 2, 2, 4, CHUNK, XD), BF16),
        pltpu.VMEM((N, CHUNK, DR), BF16),
        pltpu.VMEM((N, CHUNK, DR), BF16),
        pltpu.VMEM((N, CHUNK, 128), BF16),
        pltpu.VMEM((N, CHUNK, 128), BF16),
        pltpu.VMEM((D, HID), BF16),
        pltpu.VMEM((D, HID), BF16),
        pltpu.VMEM((HID, D), BF16),
        dma((3,)),
        dma((3,)),
        dma((N,)), dma((N,)),
        dma((N,)), dma((N,)),
        dma((2, 2, 4, 4)), dma((2, 2, 4, 4)),
        dma((2, 2, 2, 4)), dma((2, 2, 2, 4)),
        dma((N,)), dma((N,)),
        dma((N,)), dma((N,)),
        dma((3, N)),
    ]
    shapes = (
        jax.ShapeDtypeStruct((CHUNK, 128), BF16),
        jax.ShapeDtypeStruct((D, HID), BF16),
        jax.ShapeDtypeStruct((D, HID), BF16),
        jax.ShapeDtypeStruct((HID, D), BF16),
    )
    out = pl.pallas_call(
        kernel,
        out_shape=shapes,
        in_specs=[hbm] * 6,
        out_specs=(vmem, anyspace, anyspace, anyspace),
        scratch_shapes=scratch,
        compiler_params=pltpu.CompilerParams(
            collective_id=0, has_side_effects=True, vmem_limit_bytes=103 * 512 * 1024
        ),
        cost_estimate=pl.CostEstimate(
            flops=16 * 320 * D * HID, bytes_accessed=6 * D * HID * 2, transcendentals=320 * HID
        ),
    )(
        tokens.T, grad_out.T, lang_ids.T, gate_weight[0], up_weight[0], down_weight[0]
    )
    out = pl.pallas_call(
        copy_kernel,
        out_shape=shapes,
        in_specs=[vmem, anyspace, anyspace, anyspace],
        out_specs=(vmem, hbm, hbm, hbm),
        scratch_shapes=[dma((3,))],
        compiler_params=pltpu.CompilerParams(vmem_limit_bytes=8 * 1024 * 1024),
    )(*out)
    return out[0].T, out[1][None], out[2][None], out[3][None]


def solution(mesh):
    in_specs = (
        P("expert", "hidden"),
        P("expert", "hidden"),
        P("expert", None),
        P("expert", None, "hidden"),
        P("expert", None, "hidden"),
        P("expert", "hidden", None),
    )
    out_specs = (
        P("expert", "hidden"),
        P("expert", None, "hidden"),
        P("expert", None, "hidden"),
        P("expert", "hidden", None),
    )
    return jax.shard_map(local, mesh=mesh, in_specs=in_specs, out_specs=out_specs, check_vma=False)
```

time: 89.2 us -> 83.7 us (0.938)
  local copies, waits for them, and re-layouts: 5.73 us -> 2.06 us
  Pallas kernels: 82.5 us -> 80.7 us
    unnamed x10 -> x6, local copies, waits for them, and re-layouts: 5.73 us -> 2.06 us
    pallas_call x1 -> x2, Pallas kernels: 82.5 us -> 80.7 us  [the longest x1 78.7 us: local(): pl.pallas_call(kernel, out_shape=shapes, in_specs=[hbm] * 6, out_specs=(v...]
where the time goes in v2:
time: 83.7 us; the launch traced here: 83.4 us
  Pallas kernels  80.7 us (96%)
  local copies, waits for them, and re-layouts  2.06 us (2%)
    pallas_call x1, Pallas kernels, local(): pl.pallas_call(kernel, out_shape=shapes, in_specs=[hbm] * 6, out_specs=(v...  78.7 us
    unnamed x6, local copies, waits for them, and re-layouts  2.06 us
    pallas_call x1, Pallas kernels, local(): pl.pallas_call(copy_kernel, out_shape=shapes, in_specs=[vmem, anyspace, a...  2.02 us

profile of v2, /device:TPU:1, one launch (start us, length us, event | category | flops | bytes accessed | tf_op | source)
XLA Modules:
  0.0 83.4 jit_solution(9951144977283676394)
XLA Ops:
  0.6 0.0 copy-start.2
  0.6 0.6 copy-done.2
  1.3 0.0 copy-start
  1.3 0.7 copy-done
  2.0 0.0 copy-start.1
  2.0 0.7 copy-done.1
  2.7 78.7 %shard_map.93 = (bf16[48,128]{1,0:T(8,128)(2,1)S(1)}, bf16[3072,128]{1,0:T(8,128)(2,1)S(1)}, bf16[3072,128]{1,0:T(8,128)(2,1)S(1)}, bf16[128,3072]{1,0:T(8,128)(2,1)S(1)}) custom-call(bf16[48,128]{1,0:T(8,128)(2,1)S(1)} %bitcast.10, bf16[48,128]{1,0:T(8,128)(2,1)S(1)} %bitcast.11, s32[1,128]{1,0:T(1,128)S(1)} %bitcast.12, bf16[3072,128]{1,0:T(8,128)(2,1)} %bitcast.13, ...), custom_call_target="tpu_custom_call" | custom-call | flops 2013265920 | bytes 4718592 | tf_op jit(solution)/shard_map/pallas_call | solution.py:516
  81.4 2.0 %shard_map.94 = (bf16[48,128]{1,0:T(8,128)(2,1)}, bf16[3072,128]{1,0:T(8,128)(2,1)}, bf16[3072,128]{1,0:T(8,128)(2,1)}, bf16[128,3072]{1,0:T(8,128)(2,1)}) custom-call(bf16[48,128]{1,0:T(8,128)(2,1)S(1)} %get-tuple-element.12.gt, bf16[3072,128]{1,0:T(8,128)(2,1)S(1)} %get-tuple-element.13.gg, bf16[3072,128]{1,0:T(8,128)(2,1)S(1)} %get-tuple-element.14.gu, ...), custom_call_target="tpu_custom_call" | custom-call | tf_op jit(solution)/shard_map/pallas_call | solution.py:531
Async XLA Ops:
  0.6 0.7 copy-start.2
  1.3 0.7 copy-start
  2.0 0.7 copy-start.1

commit v3 on v2

--- a/solution.py
+++ b/solution.py
@@ -16,6 +16,7 @@
 D = 64 * CHUNK
 MAIN = 256
 XD = 640
+PART = 16
 DR = 384
 
 
@@ -39,24 +40,20 @@
     return 2 * i - 4 + odd
 
 
-ORDER = (2, 1, 3, 0)
+MESSAGES = (
+    ((4, 1, ()), (2, 1, ()), (3, 2, (0,)), (1, 1, (1, 2))),
+    ((3, 1, ()), (2, 1, (0,)), (1, 1, (1,))),
+)
 PEERS = (4, 3, 5, 2, 6, 1, 7)
 
 
 def kernel(
-    x_hbm, dy_hbm, lang_hbm, wg_hbm, wu_hbm, wd_hbm,
+    tok_ref, wg_hbm, wu_hbm, wd_hbm,
     gt_ref, gg_hbm, gu_hbm, gd_hbm,
-    x_ref, dy_ref, lang_ref, wg, wu, wd, wdt, msg, blk, xd, place, oht, acc_gu, acc_d, acc_t, gcat, hcat,
+    wg, wu, wd, wdt, msg, blk, xd, place, oht, acc_gu, acc_d, acc_t, gcat, hcat,
     part, rsend, rrecv, ssend, srecv, bsend, brecv, gg, gu, gd,
-    tsem, wsem, a_s, a_r, m_s, m_r, g_s, g_r, r_s, r_r, s_s, s_r, b_s, b_r, osem,
+    wsem, a_s, a_r, m_s, m_r, g_s, g_r, r_s, r_r, s_s, s_r, b_s, b_r, osem,
 ):
-    tok = [
-        pltpu.make_async_copy(src, dst, tsem.at[k])
-        for k, (src, dst) in enumerate(((lang_hbm, lang_ref), (x_hbm, x_ref), (dy_hbm, dy_ref)))
-    ]
-    for c in tok:
-        c.start()
-
     e = lax.axis_index("expert")
     hid = lax.axis_index("hidden")
     core = lax.rem(e, 2)
@@ -67,21 +64,29 @@
     def wrap(v):
         return lax.rem(v + 2 * N, N)
 
-    def way_of(q):
-        return lax.rem(own + q, 2)
-
-    def first(q):
-        c = way_of(q)
-        return y * (1 - c) + z * c
+    at = (y + own * (z - y), z + own * (y - z))
+    stride = (N - 7 * own, 1 + 7 * own)
+    table = [[wrap(at[q] + k) * stride[q] for k in range(N)] for q in (0, 1)]
+    sides = [[lax.rem((at[q] + odd) // 2, 2) for odd in (0, 1)] for q in (0, 1)]
+
+    def along(q, d):
+        if isinstance(d, int):
+            return table[q][d % N]
+        return wrap(at[q] + d) * stride[q]
 
     def hx(q, du, dv):
-        c = way_of(q)
-        u = wrap(y * (1 - c) + z * c + du)
-        v = wrap(z * (1 - c) + y * c + dv)
-        return u * (N - 7 * c) + v * (1 + 7 * c)
+        return along(q, du) + along(1 - q, dv)
 
     def side(q, odd):
-        return lax.rem((first(q) + odd) // 2, 2)
+        return sides[q][odd]
+
+    def either(sel, values):
+        return values[0] + sel * (values[1] - values[0])
+
+    def chunk_of(q, sel, i, odd, dv):
+        if isinstance(sel, int):
+            return hx(q, off(i + sel, odd), dv)
+        return either(sel, [along(q, off(i + k, odd)) for k in (0, 1)]) + along(1 - q, dv)
 
     def rows(h):
         return pl.ds(pl.multiple_of(h * CHUNK, CHUNK), CHUNK)
@@ -92,11 +97,12 @@
         )
 
     bar = pltpu.get_barrier_semaphore()
-    for j in range(1, N):
+    for j in PEERS:
+        pl.semaphore_signal(bar, inc=1, device_id={"hidden": hx(0, j, 0)}, device_id_type=MESH)
+        if j != 4:
+            pl.semaphore_signal(bar, inc=1, device_id={"hidden": hx(1, j, 0)}, device_id_type=MESH)
+    for j in PEERS:
         pl.semaphore_signal(bar, inc=1, device_id={"expert": wrap(e + j)}, device_id_type=MESH)
-        pl.semaphore_signal(bar, inc=1, device_id={"hidden": hx(0, j, 0)}, device_id_type=MESH)
-    for j in (1, -1, 3, -3):
-        pl.semaphore_signal(bar, inc=1, device_id={"hidden": hx(1, j, 0)}, device_id_type=MESH)
 
     loads = [
         pltpu.make_async_copy(src, dst, wsem.at[k])
@@ -104,16 +110,14 @@
     ]
     for c in loads:
         c.start()
-    for c in tok:
-        c.wait()
-
-    lang = lang_ref[...]
+
+    lang = tok_ref[2 * CHUNK : 2 * CHUNK + 1, :].astype(jnp.int32)
     member = iota((N, 128), 0) == lang
     earlier = (iota((128, 128), 0) < iota((128, 128), 1)).astype(BF16)
     before = nn(member.astype(BF16), earlier)
     slot = jnp.sum(jnp.where(member, before, 0.0), axis=0, keepdims=True).astype(jnp.int32)
     oht[...] = (iota((N * 64, 128), 0) == lang * 64 + slot).astype(BF16)
-    out = nt(jnp.concatenate([x_ref[...], dy_ref[...]], axis=0), oht[...])
+    out = nt(tok_ref[0 : 2 * CHUNK, :].astype(BF16), oht[...])
     low = iota((CHUNK, 128), 1) < 64
     for k in range(N):
         tile = slice(k // 2 * 128, k // 2 * 128 + 128)
@@ -124,7 +128,7 @@
             x_k = pltpu.roll(x_k, 64, 1)
         msg[k] = jnp.where(low, x_k, dy_k).astype(BF16)
 
-    pl.semaphore_wait(bar, 2 * (N - 1) + 4)
+    pl.semaphore_wait(bar, 2 * (N - 1) + 6)
 
     def to_expert(j, src, dst, ss, rs):
         return remote(src.at[wrap(e + j)], dst.at[e], ss.at[j], rs.at[j], {"expert": wrap(e + j)})
@@ -164,29 +168,26 @@
         h = hx(k % 2, k, 0)
         remote(xd.at[h], xd.at[h], m_s.at[k], m_r.at[k], {"hidden": hid}).wait_recv()
 
-    def big(q, i, d, s):
+    def big(q, i, d, s, sel=0):
         to = 1 - 2 * d
-        h = hx(q, off(i, (s + q) % 2), -to * s)
-        c = way[q]
+        h = chunk_of(q, sel, i, (s + q) % 2, -to * s)
+        c, i = way[q], i + sel
         return remote(
             xd.at[h], xd.at[h], g_s.at[c, d, s, i], g_r.at[c, d, s, i], {"hidden": hx(q, 0, to)}
         )
 
-    def big_recv(q, i, d, s):
+    def big_recv(q, i, d, s, sel=0):
         to = 1 - 2 * d
-        h = hx(q, off(i, (s + 1 + q) % 2), -to * (s + 1))
-        c = way[q]
+        h = chunk_of(q, sel, i, (s + 1 + q) % 2, -to * (s + 1))
+        c, i = way[q], i + sel
         remote(xd.at[h], xd.at[h], g_s.at[c, d, s, i], g_r.at[c, d, s, i], {"hidden": hid}).wait_recv()
 
     def goes_far(q, d, s):
         c = side(q, (s + q) % 2)
-        c = c if d == 0 else 1 - c
-        return [c, c + 2]
+        return c if d == 0 else 1 - c
 
     def stays(q, d, s):
-        c = side(q, (s + q) % 2)
-        c = 1 - c if d == 0 else c
-        return [c, c + 2]
+        return 1 - goes_far(q, d, s)
 
     def send_big(q, i, s):
         for d in (0, 1):
@@ -214,7 +215,6 @@
     relay[2].start()
     send_big(0, 3, 0)
     send_big(0, 1, 0)
-    send_big(1, 2, 1)
     small_recv(3)
     send_big(1, 3, 0)
     small_recv(5)
@@ -237,21 +237,24 @@
     forward(column(0))
     for s in range(1, 4):
         if s < 3:
-            for i in ORDER:
-                for q in (0, 1):
-                    if (s, q, i) != (1, 1, 2):
-                        send_big(q, i, s)
+            for pick in (goes_far, stays):
+                for j in (1, 0):
+                    for q in (0, 1):
+                        for d in (0, 1):
+                            sel = pick(q, d, s)
+                            big_recv(q, 2 * j, d, s - 1, sel)
+                            big(q, 2 * j, d, s, sel).start()
         else:
             for j in (0, 1):
                 for q in (0, 1):
                     for d in (0, 1):
-                        i = goes_far(q, d, 3)[j]
-                        big_recv(q, i, d, 2)
-                        big(q, i, d, 3).start()
+                        sel = goes_far(q, d, 3)
+                        big_recv(q, 2 * j, d, 2, sel)
+                        big(q, 2 * j, d, 3, sel).start()
             for q in (0, 1):
                 for d in (0, 1):
-                    for i in stays(q, d, 3):
-                        big_recv(q, i, d, 2)
+                    for j in (0, 1):
+                        big_recv(q, 2 * j, d, 2, stays(q, d, 3))
 
         def two(k, carry):
             forward(column((1 - 2 * k) * s))
@@ -261,8 +264,8 @@
 
     for q in (0, 1):
         for d in (0, 1):
-            for i in goes_far(q, d, 4):
-                big_recv(q, i, d, 3)
+            for j in (0, 1):
+                big_recv(q, 2 * j, d, 3, goes_far(q, d, 4))
     forward(column(4))
 
     def units(gate, up, dh):
@@ -299,42 +302,40 @@
             part[h, :, 0:MAIN] = block[:, 0:MAIN]
             part[h, :, MAIN:DR] = block[:, MAIN:DR] if n % 4 < 2 else block[:, DR : DR + 128]
 
-    def reduce_copy(q, d, short, s):
-        c = way[q]
+    def reduce_copy(q, d, short, m, n):
+        place = (way[q], d, short, m, n)
+        hops = MESSAGES[short][m][1] if isinstance(m, int) else 1
+        to = hops * (1 - 2 * d)
         return remote(
-            rsend.at[c, d, short, s],
-            rrecv.at[c, d, short, s],
-            r_s.at[c, d, short, s],
-            r_r.at[c, d, short, s],
-            {"hidden": hx(q, 0, 1 - 2 * d)},
+            rsend.at[place], rrecv.at[place], r_s.at[place], r_r.at[place], {"hidden": hx(q, 0, to)}
         )
 
-    def pair_parts(q, sel, odd, dist):
-        h0, h1 = hx(q, off(sel, odd), dist), hx(q, off(sel + 2, odd), dist)
-        return [part[h0, :, 0:MAIN], part[h1, :, 0:MAIN], part[h0, :, MAIN:DR] + part[h1, :, MAIN:DR]]
+    def pair_parts(q, sel, odd, dist, span):
+        h0, h1 = [chunk_of(q, sel, i, odd, dist) for i in (0, 2)]
+        return [part[h0, span, 0:MAIN], part[h1, span, 0:MAIN], part[h0, span, MAIN:DR] + part[h1, span, MAIN:DR]]
 
     def add_message(values, message):
         spans = ((0, MAIN), (MAIN, 2 * MAIN), (2 * MAIN, XD))
         return [v + message[:, lo:hi].astype(F32) for v, (lo, hi) in zip(values, spans)]
 
-    def reduce_step(q, d, short, s):
-        left_hops = 4 - short - s
-        odd = (q + left_hops) % 2
+    def reduce_step(q, d, short, m, n):
+        dist, _, merged = MESSAGES[short][m]
+        odd = (q + dist) % 2
         sel = side(q, odd)
         sel = sel if d == short else 1 - sel
-        values = pair_parts(q, sel, odd, (1 - 2 * d) * left_hops)
+        values = pair_parts(q, sel, odd, (1 - 2 * d) * dist, slice(n * PART, (n + 1) * PART))
         c = way[q]
-        if s > 0:
-            reduce_copy(q, d, short, s - 1).wait_recv()
-            values = add_message(values, rrecv[c, d, short, s - 1])
-        rsend[c, d, short, s] = jnp.concatenate([v.astype(BF16) for v in values], axis=1)
-        reduce_copy(q, d, short, s).start()
-
-    def reduce_stage(s, pick):
-        for short in pick:
+        for k in merged:
+            reduce_copy(q, d, short, k, n).wait_recv()
+            values = add_message(values, rrecv[c, d, short, k, n])
+        rsend[c, d, short, m, n] = jnp.concatenate([v.astype(BF16) for v in values], axis=1)
+        reduce_copy(q, d, short, m, n).start()
+
+    def reduce_send(short, m):
+        for n in range(CHUNK // PART):
             for q in (0, 1):
                 for d in (0, 1):
-                    reduce_step(q, d, short, s)
+                    reduce_step(q, d, short, m, n)
 
     def weight_grads(g):
         span = pl.ds(pl.multiple_of(g * N * CHUNK, N * CHUNK), N * CHUNK)
@@ -357,40 +358,40 @@
         lax.fori_loop(lo, hi, one, 0)
 
     partial_sums(4)
-    reduce_stage(0, (0,))
-    partial_sums(3)
-    partial_sums(-3)
-    reduce_stage(0, (1,))
-
-    def rest(k, carry):
-        partial_sums(k - 2)
-        return carry
-
-    lax.fori_loop(0, 5, rest, 0)
-    reduce_stage(1, (0, 1))
-    grads(0, 3)
-    reduce_stage(2, (0, 1))
-    grads(3, 6)
-    reduce_stage(3, (0,))
-    grads(6, 8)
+    reduce_send(0, 0)
+
+    def near(dist):
+        def both(k, carry):
+            partial_sums((1 - 2 * k) * dist)
+            return carry
+
+        lax.fori_loop(0, 2, both, 0)
+
+    near(3)
+    reduce_send(1, 0)
+    near(2)
+    reduce_send(0, 1)
+    near(1)
+    partial_sums(0)
+    reduce_send(0, 2)
+    reduce_send(1, 1)
+    grads(0, 4)
+    reduce_send(0, 3)
+    reduce_send(1, 2)
+    grads(4, 8)
 
     def small_sum(k, q):
         return remote(ssend.at[k], srecv.at[k], s_s.at[k], s_r.at[k], {"hidden": hx(q, k, 0)})
 
-    for q, sel in ((1, 0), (1, 1), (0, 1), (0, 0)):
+    for q, sel in ((0, 0), (1, 0), (1, 1), (0, 1)):
         bit = lax.rem(side(q, q) + sel, 2)
         c = way[q]
-        values = pair_parts(q, sel, q, 0)
+        values = pair_parts(q, sel, q, 0, slice(0, CHUNK))
         for d, short in ((0, bit), (1, 1 - bit)):
             last = 3 - short
-            remote(
-                rsend.at[c, d, short, last],
-                rrecv.at[c, d, short, last],
-                r_s.at[c, d, short, last],
-                r_r.at[c, d, short, last],
-                {"hidden": hid},
-            ).wait_recv()
-            values = add_message(values, rrecv[c, d, short, last])
+            for n in range(CHUNK // PART):
+                reduce_copy(q, d, short, last, n).wait_recv()
+            values = add_message(values, rrecv[c, d, short, last].reshape(CHUNK, XD))
         for j in (0, 1):
             k = off(sel + 2 * j, q) % N
             if k == 0:
@@ -429,11 +430,12 @@
             for s in range(3):
                 for i in range(4):
                     big(q, i, d, s).wait_send()
-            for i in goes_far(q, d, 3):
-                big(q, i, d, 3).wait_send()
+            for j in (0, 1):
+                big(q, 2 * j, d, 3, goes_far(q, d, 3)).wait_send()
             for short in (0, 1):
                 for s in range(4 - short):
-                    reduce_copy(q, d, short, s).wait_send()
+                    for n in range(CHUNK // PART):
+                        reduce_copy(q, d, short, s, n).wait_send()
     for k in range(1, N):
         small_sum(k, k % 2).wait_send()
 
@@ -470,9 +472,6 @@
     hbm = pl.BlockSpec(memory_space=pltpu.HBM)
     dma = pltpu.SemaphoreType.DMA
     scratch = [
-        pltpu.VMEM((CHUNK, 128), BF16),
-        pltpu.VMEM((CHUNK, 128), BF16),
-        pltpu.VMEM((1, 128), jnp.int32),
         pltpu.VMEM((D, HID), BF16),
         pltpu.VMEM((D, HID), BF16),
         pltpu.VMEM((HID, D), BF16),
@@ -488,8 +487,8 @@
         pltpu.VMEM((2 * HID, DR + 128), BF16),
         pltpu.VMEM((HID, DR), BF16),
         pltpu.VMEM((64, CHUNK, DR), F32),
-        pltpu.VMEM((2, 2, 2, 4, CHUNK, XD), BF16),
-        pltpu.VMEM((2, 2, 2, 4, CHUNK, XD), BF16),
+        pltpu.VMEM((2, 2, 2, 4, CHUNK // PART, PART, XD), BF16),
+        pltpu.VMEM((2, 2, 2, 4, CHUNK // PART, PART, XD), BF16),
         pltpu.VMEM((N, CHUNK, DR), BF16),
         pltpu.VMEM((N, CHUNK, DR), BF16),
         pltpu.VMEM((N, CHUNK, 128), BF16),
@@ -498,15 +497,15 @@
         pltpu.VMEM((D, HID), BF16),
         pltpu.VMEM((HID, D), BF16),
         dma((3,)),
-        dma((3,)),
         dma((N,)), dma((N,)),
         dma((N,)), dma((N,)),
         dma((2, 2, 4, 4)), dma((2, 2, 4, 4)),
-        dma((2, 2, 2, 4)), dma((2, 2, 2, 4)),
+        dma((2, 2, 2, 4, CHUNK // PART)), dma((2, 2, 2, 4, CHUNK // PART)),
         dma((N,)), dma((N,)),
         dma((N,)), dma((N,)),
         dma((3, N)),
     ]
+    packed = jnp.concatenate([v.T.astype(F32) for v in (tokens, grad_out, lang_ids)], axis=0)
     shapes = (
         jax.ShapeDtypeStruct((CHUNK, 128), BF16),
         jax.ShapeDtypeStruct((D, HID), BF16),
@@ -516,7 +515,7 @@
     out = pl.pallas_call(
         kernel,
         out_shape=shapes,
-        in_specs=[hbm] * 6,
+        in_specs=[vmem] + [hbm] * 3,
         out_specs=(vmem, anyspace, anyspace, anyspace),
         scratch_shapes=scratch,
         compiler_params=pltpu.CompilerParams(
@@ -526,7 +525,7 @@
             flops=16 * 320 * D * HID, bytes_accessed=6 * D * HID * 2, transcendentals=320 * HID
         ),
     )(
-        tokens.T, grad_out.T, lang_ids.T, gate_weight[0], up_weight[0], down_weight[0]
+        packed, gate_weight[0], up_weight[0], down_weight[0]
     )
     out = pl.pallas_call(
         copy_kernel,

time: 83.7 us -> 81.4 us (0.973)
  Pallas kernels: 80.7 us -> 79.1 us
  local copies, waits for them, and re-layouts: 2.06 us -> 0.65 us
    pallas_call x1, Pallas kernels: 78.7 us -> 77.1 us  [local(): pl.pallas_call(kernel, out_shape=shapes, in_specs=[vmem] + [hbm] * 3, out...]
    unnamed x6 -> x2, local copies, waits for them, and re-layouts: 2.06 us -> 0.65 us
where the time goes in v3:
time: 81.4 us; the launch traced here: 81.1 us
  Pallas kernels  79.1 us (97%)
    pallas_call x1, Pallas kernels, local(): pl.pallas_call(kernel, out_shape=shapes, in_specs=[vmem] + [hbm] * 3, out...  77.1 us
    pallas_call x1, Pallas kernels, local(): pl.pallas_call(copy_kernel, out_shape=shapes, in_specs=[vmem, anyspace, a...  2.02 us

profile of v3, /device:TPU:1, one launch (start us, length us, event | category | flops | bytes accessed | tf_op | source)
XLA Modules:
  0.0 81.1 jit_solution(1909186587407373484)
XLA Ops:
  0.6 0.0 copy-start
  0.6 0.6 copy-done
  1.3 0.7 convert_bitcast_fusion
  2.0 77.1 %shard_map.93 = (bf16[48,128]{1,0:T(8,128)(2,1)S(1)}, bf16[3072,128]{1,0:T(8,128)(2,1)S(1)}, bf16[3072,128]{1,0:T(8,128)(2,1)S(1)}, bf16[128,3072]{1,0:T(8,128)(2,1)S(1)}) custom-call(f32[97,128]{1,0:T(8,128)S(1)} %pad_maximum_fusion.tok_ref, bf16[3072,128]{1,0:T(8,128)(2,1)} %bitcast.13, bf16[3072,128]{1,0:T(8,128)(2,1)} %bitcast.14, bf16[128,3072]{1,0:T(8,128)(2,1)} %bitcast.15), custom_call_target="tpu_custom_call" | custom-call | flops 2013265920 | bytes 4718592 | tf_op jit(solution)/shard_map/pallas_call | solution.py:515
  79.1 2.0 %shard_map.94 = (bf16[48,128]{1,0:T(8,128)(2,1)}, bf16[3072,128]{1,0:T(8,128)(2,1)}, bf16[3072,128]{1,0:T(8,128)(2,1)}, bf16[128,3072]{1,0:T(8,128)(2,1)}) custom-call(bf16[48,128]{1,0:T(8,128)(2,1)S(1)} %get-tuple-element.12.gt, bf16[3072,128]{1,0:T(8,128)(2,1)S(1)} %get-tuple-element.13.gg, bf16[3072,128]{1,0:T(8,128)(2,1)S(1)} %get-tuple-element.14.gu, ...), custom_call_target="tpu_custom_call" | custom-call | tf_op jit(solution)/shard_map/pallas_call | solution.py:530
  (2 shorter events, 0.0 us)
Async XLA Ops:
  0.6 0.7 copy-start

commit v4 on v3

--- a/solution.py
+++ b/solution.py
@@ -16,7 +16,7 @@
 D = 64 * CHUNK
 MAIN = 256
 XD = 640
-PART = 16
+PART = 48
 DR = 384
 
 
@@ -48,7 +48,7 @@
 
 
 def kernel(
-    tok_ref, wg_hbm, wu_hbm, wd_hbm,
+    tok_ref, lang_ref, wg_hbm, wu_hbm, wd_hbm,
     gt_ref, gg_hbm, gu_hbm, gd_hbm,
     wg, wu, wd, wdt, msg, blk, xd, place, oht, acc_gu, acc_d, acc_t, gcat, hcat,
     part, rsend, rrecv, ssend, srecv, bsend, brecv, gg, gu, gd,
@@ -111,13 +111,13 @@
     for c in loads:
         c.start()
 
-    lang = tok_ref[2 * CHUNK : 2 * CHUNK + 1, :].astype(jnp.int32)
+    lang = lang_ref[...]
     member = iota((N, 128), 0) == lang
     earlier = (iota((128, 128), 0) < iota((128, 128), 1)).astype(BF16)
     before = nn(member.astype(BF16), earlier)
     slot = jnp.sum(jnp.where(member, before, 0.0), axis=0, keepdims=True).astype(jnp.int32)
     oht[...] = (iota((N * 64, 128), 0) == lang * 64 + slot).astype(BF16)
-    out = nt(tok_ref[0 : 2 * CHUNK, :].astype(BF16), oht[...])
+    out = nt(tok_ref[...].astype(BF16), oht[...])
     low = iota((CHUNK, 128), 1) < 64
     for k in range(N):
         tile = slice(k // 2 * 128, k // 2 * 128 + 128)
@@ -147,16 +147,8 @@
     lane = jnp.where(jj < CAP, lane, -1)
     place[...] = (iota((N * 128, XD), 1) == lane).astype(BF16)
 
-    for c in loads:
-        c.wait()
-    for k in range(D // 128):
-        wdt[pl.ds(k * 128, 128), :] = wd[:, k * 128 : (k + 1) * 128].T
-    acc_gu[...] = jnp.zeros_like(acc_gu)
-    acc_d[...] = jnp.zeros_like(acc_d)
-    acc_t[...] = jnp.zeros_like(acc_t)
-
     for c in a2a:
-        c.wait()
+        c.wait_recv()
     cat = jnp.concatenate([blk[k] for k in range(N)], axis=1)
     xd[hid] = nn(cat, place[...]).astype(BF16)
 
@@ -204,6 +196,13 @@
     send_big(0, 2, 0)
     sends[2].start()
     sends[3].start()
+    for c in loads:
+        c.wait()
+    for k in range(D // 128):
+        wdt[pl.ds(k * 128, 128), :] = wd[:, k * 128 : (k + 1) * 128].T
+    acc_gu[...] = jnp.zeros_like(acc_gu)
+    acc_d[...] = jnp.zeros_like(acc_d)
+    acc_t[...] = jnp.zeros_like(acc_t)
     small_recv(1)
     send_big(1, 2, 0)
     small_recv(7)
@@ -399,6 +398,21 @@
             else:
                 ssend[k] = jnp.concatenate([values[j].astype(BF16), values[2].astype(BF16)], axis=1)
                 small_sum(k, q).start()
+    for c in a2a:
+        c.wait_send()
+    for c in sends + relay:
+        c.wait_send()
+    for q in (0, 1):
+        for d in (0, 1):
+            for s in range(3):
+                for i in range(4):
+                    big(q, i, d, s).wait_send()
+            for j in (0, 1):
+                big(q, 2 * j, d, 3, goes_far(q, d, 3)).wait_send()
+            for short in (0, 1):
+                for s in range(4 - short):
+                    for n in range(CHUNK // PART):
+                        reduce_copy(q, d, short, s, n).wait_send()
     low_sum = jnp.zeros((CHUNK, 128), F32)
 
     p_i = iota((DR, N * 128), 0)
@@ -423,22 +437,8 @@
         c.start()
     brecv[e] = bsend[e]
 
-    for c in sends + relay:
-        c.wait_send()
-    for q in (0, 1):
-        for d in (0, 1):
-            for s in range(3):
-                for i in range(4):
-                    big(q, i, d, s).wait_send()
-            for j in (0, 1):
-                big(q, 2 * j, d, 3, goes_far(q, d, 3)).wait_send()
-            for short in (0, 1):
-                for s in range(4 - short):
-                    for n in range(CHUNK // PART):
-                        reduce_copy(q, d, short, s, n).wait_send()
     for k in range(1, N):
         small_sum(k, k % 2).wait_send()
-
     def flush(g, carry):
         span = pl.ds(pl.multiple_of(g * N * CHUNK, N * CHUNK), N * CHUNK)
         for k, (src, dst) in enumerate(((gg, gg_hbm), (gu, gu_hbm))):
@@ -447,7 +447,6 @@
         return carry
 
     lax.fori_loop(0, N, flush, 0)
-
     for c in home:
         c.wait()
     cat = jnp.concatenate([jnp.where(low, brecv[k], brecv[k + 1]) for k in range(0, N, 2)], axis=1)
@@ -505,7 +504,7 @@
         dma((N,)), dma((N,)),
         dma((3, N)),
     ]
-    packed = jnp.concatenate([v.T.astype(F32) for v in (tokens, grad_out, lang_ids)], axis=0)
+    packed = jnp.concatenate([v.T.astype(F32) for v in (tokens, grad_out)], axis=0)
     shapes = (
         jax.ShapeDtypeStruct((CHUNK, 128), BF16),
         jax.ShapeDtypeStruct((D, HID), BF16),
@@ -515,7 +514,7 @@
     out = pl.pallas_call(
         kernel,
         out_shape=shapes,
-        in_specs=[vmem] + [hbm] * 3,
+        in_specs=[vmem] * 2 + [hbm] * 3,
         out_specs=(vmem, anyspace, anyspace, anyspace),
         scratch_shapes=scratch,
         compiler_params=pltpu.CompilerParams(
@@ -525,7 +524,7 @@
             flops=16 * 320 * D * HID, bytes_accessed=6 * D * HID * 2, transcendentals=320 * HID
         ),
     )(
-        packed, gate_weight[0], up_weight[0], down_weight[0]
+        packed, lang_ids.T, gate_weight[0], up_weight[0], down_weight[0]
     )
     out = pl.pallas_call(
         copy_kernel,

time: 81.4 us -> 80.6 us (level)
  no operation moved by 1% of the time
where the time goes in v4:
time: 80.6 us; the launch traced here: 80.4 us
  Pallas kernels  79.1 us (98%)
    pallas_call x1, Pallas kernels, local(): pl.pallas_call(kernel, out_shape=shapes, in_specs=[vmem] * 2 + [hbm] * 3,...  77 us
    pallas_call x1, Pallas kernels, local(): pl.pallas_call(copy_kernel, out_shape=shapes, in_specs=[vmem, anyspace, a...  2.02 us

profile of v4, /device:TPU:1, one launch (start us, length us, event | category | flops | bytes accessed | tf_op | source)
XLA Modules:
  0.0 80.4 jit_solution(1909505494859817653)
XLA Ops:
  0.6 0.0 copy-start
  0.6 0.7 maximum_convert_fusion.tok_ref
  1.4 0.0 copy-done
  1.4 77.0 %shard_map.93 = (bf16[48,128]{1,0:T(8,128)(2,1)S(1)}, bf16[3072,128]{1,0:T(8,128)(2,1)S(1)}, bf16[3072,128]{1,0:T(8,128)(2,1)S(1)}, bf16[128,3072]{1,0:T(8,128)(2,1)S(1)}) custom-call(f32[96,128]{1,0:T(8,128)S(1)} %maximum_convert_fusion.tok_ref, s32[1,128]{1,0:T(1,128)S(1)} %bitcast.10, bf16[3072,128]{1,0:T(8,128)(2,1)} %bitcast.13, ...), custom_call_target="tpu_custom_call" | custom-call | flops 2013265920 | bytes 4718592 | tf_op jit(solution)/shard_map/pallas_call | solution.py:514
  78.4 2.0 %shard_map.94 = (bf16[48,128]{1,0:T(8,128)(2,1)}, bf16[3072,128]{1,0:T(8,128)(2,1)}, bf16[3072,128]{1,0:T(8,128)(2,1)}, bf16[128,3072]{1,0:T(8,128)(2,1)}) custom-call(bf16[48,128]{1,0:T(8,128)(2,1)S(1)} %get-tuple-element.12.gt, bf16[3072,128]{1,0:T(8,128)(2,1)S(1)} %get-tuple-element.13.gg, bf16[3072,128]{1,0:T(8,128)(2,1)S(1)} %get-tuple-element.14.gu, ...), custom_call_target="tpu_custom_call" | custom-call | tf_op jit(solution)/shard_map/pallas_call | solution.py:529
Async XLA Ops:
  0.6 0.7 copy-start

commit v5 on v4

--- a/solution.py
+++ b/solution.py
@@ -147,10 +147,14 @@
     lane = jnp.where(jj < CAP, lane, -1)
     place[...] = (iota((N * 128, XD), 1) == lane).astype(BF16)
 
-    for c in a2a:
+    def placed(k):
+        return nn(blk[k], place[pl.ds(pl.multiple_of(k * 128, 128), 128), :])
+
+    chunk = placed(e)
+    for j, c in zip(reversed(PEERS), reversed(a2a)):
         c.wait_recv()
-    cat = jnp.concatenate([blk[k] for k in range(N)], axis=1)
-    xd[hid] = nn(cat, place[...]).astype(BF16)
+        chunk = chunk + placed(wrap(e - j))
+    xd[hid] = chunk.astype(BF16)
 
     def small(k, q, chunk, to):
         h = hx(q, chunk, 0)

time: 80.6 us -> 80.8 us (level)
  no operation moved by 1% of the time
where the time goes in v5:
time: 80.8 us; the launch traced here: 80.6 us
  Pallas kernels  79.2 us (98%)
    pallas_call x1, Pallas kernels, local(): pl.pallas_call(kernel, out_shape=shapes, in_specs=[vmem] * 2 + [hbm] * 3,...  77.2 us
    pallas_call x1, Pallas kernels, local(): pl.pallas_call(copy_kernel, out_shape=shapes, in_specs=[vmem, anyspace, a...  2.02 us

profile of v5, /device:TPU:1, one launch (start us, length us, event | category | flops | bytes accessed | tf_op | source)
XLA Modules:
  0.0 80.6 jit_solution(542308553109927837)
XLA Ops:
  0.6 0.0 copy-start
  0.6 0.7 maximum_convert_fusion.tok_ref
  1.4 0.0 copy-done
  1.4 77.2 %shard_map.93 = (bf16[48,128]{1,0:T(8,128)(2,1)S(1)}, bf16[3072,128]{1,0:T(8,128)(2,1)S(1)}, bf16[3072,128]{1,0:T(8,128)(2,1)S(1)}, bf16[128,3072]{1,0:T(8,128)(2,1)S(1)}) custom-call(f32[96,128]{1,0:T(8,128)S(1)} %maximum_convert_fusion.tok_ref, s32[1,128]{1,0:T(1,128)S(1)} %bitcast.10, bf16[3072,128]{1,0:T(8,128)(2,1)} %bitcast.13, ...), custom_call_target="tpu_custom_call" | custom-call | flops 2013265920 | bytes 4718592 | tf_op jit(solution)/shard_map/pallas_call | solution.py:518
  78.6 2.0 %shard_map.94 = (bf16[48,128]{1,0:T(8,128)(2,1)}, bf16[3072,128]{1,0:T(8,128)(2,1)}, bf16[3072,128]{1,0:T(8,128)(2,1)}, bf16[128,3072]{1,0:T(8,128)(2,1)}) custom-call(bf16[48,128]{1,0:T(8,128)(2,1)S(1)} %get-tuple-element.12.gt, bf16[3072,128]{1,0:T(8,128)(2,1)S(1)} %get-tuple-element.13.gg, bf16[3072,128]{1,0:T(8,128)(2,1)S(1)} %get-tuple-element.14.gu, ...), custom_call_target="tpu_custom_call" | custom-call | tf_op jit(solution)/shard_map/pallas_call | solution.py:533
Async XLA Ops:
  0.6 0.7 copy-start
